TPU v7x, 128 devices: a whole 4x4x4 slice. The times are simulated.
128 devices in a mesh: role: 2 (over y_lo), grp: 64 (over y_hi, z, x, core).
Axes of the slice: x: 4, y: 4 (y_hi: 2, y_lo: 2; y = y_hi * 2 + y_lo), z: 4, core: 2. Of those that a mesh axis runs over, the one named last changes fastest.
Arguments:
- hidden_state: float32 [128, 8192], P(None, ('role', 'grp')), may hold values from -6 to 6
- gain_attn: float32 [8192], P(('role', 'grp')), may hold values from 0.25 to 1.75
- gain_ffn: float32 [8192], P(('role', 'grp')), may hold values from 0.25 to 1.75
- w_qkv: bfloat16 [9216, 8192], P(('role', 'grp')), may hold values from -0.0625 to 0.0625
- w_out: bfloat16 [8192, 8192], P(('role', 'grp')), may hold values from -0.0625 to 0.0625
- w_gate: bfloat16 [53248, 8192], P(('role', 'grp')), may hold values from -0.0625 to 0.0625
- w_up: bfloat16 [53248, 8192], P(('role', 'grp')), may hold values from -0.0625 to 0.0625
- w_down: bfloat16 [53248, 8192], P(('role', 'grp')), may hold values from -0.02734375 to 0.02734375
- kv_cache: bfloat16 [128, 1024, 1024], P(('role', 'grp'))
- lengths: int32 [128], replicated, may hold values from 1 to 1024, as said below
- row_order: int32 [128], replicated, may hold values from 0 to 127, each once
Outputs:
- out_state: float32 [128, 8192], P(None, ('role', 'grp'))
Inputs may be any that keep to these rules, and one draw needn't show every extreme that they name: `lengths`: every sequence has at least one cached position; some sequence has all 1024. `row_order`: each sequence is named by exactly one cache row.
All inputs are finite; a program needn't handle non-finite values.
Results may differ from a plain program's by a relative error of at most 0.0099.
Values may be sent and summed in bfloat16 or wider, within the bound.
A program may use at most 128 MiB of HBM per device.

v0:
```python
import jax
import jax.numpy as jnp
from jax import lax
from jax.sharding import PartitionSpec as P

QH = 64
KVH = 4
HD = 128


def contract_rows(left, right):
    return lax.dot_general(
        left, right, (((1,), (1,)), ((), ())), preferred_element_type=jnp.float32
    )


def per_device(
    hidden_state,
    gain_attn,
    gain_ffn,
    w_qkv,
    w_out,
    w_gate,
    w_up,
    w_down,
    kv_cache,
    lengths,
    row_order,
):
    place = lax.axis_index("role") * lax.axis_size("grp") + lax.axis_index("grp")
    total_rows = hidden_state.shape[0]
    owned = kv_cache.shape[0]
    length = kv_cache.shape[1]
    key_width = KVH * HD
    query_width = QH * HD
    groups = QH // KVH
    scale = 1.0 / HD**0.5
    inverse = (
        jnp.zeros((total_rows,), jnp.int32)
        .at[row_order]
        .set(jnp.arange(total_rows, dtype=jnp.int32))
    )
    slot_lens = lax.dynamic_slice_in_dim(lengths[row_order], place * owned, owned)
    valid = (jnp.arange(length, dtype=jnp.int32)[None, :] < slot_lens[:, None])[:, None, None, :]
    keys = kv_cache[:, :, :key_width].reshape(owned, length, KVH, HD)
    values = kv_cache[:, :, key_width:].reshape(owned, length, KVH, HD)

    def full_normed(state, gain):
        whole, whole_gain = (
            lax.all_gather(state, ("role", "grp"), axis=1, tiled=True),
            lax.all_gather(gain, ("role", "grp"), axis=0, tiled=True),
        )
        mean = jnp.mean(whole * whole, axis=1, keepdims=True)
        return (whole * lax.rsqrt(mean + 1e-05) * whole_gain).astype(jnp.bfloat16)

    state = hidden_state
    normed_a = full_normed(state, gain_attn)
    projected = contract_rows(normed_a, w_qkv).astype(jnp.bfloat16)
    mine = lax.all_to_all(
        projected[row_order], ("role", "grp"), split_axis=0, concat_axis=1, tiled=True
    )
    recent = [mine[:, query_width:]]
    query = mine[:, :query_width]
    query = query.reshape(owned, KVH, groups, HD)
    fresh_all = jnp.stack(recent, axis=1)
    count = fresh_all.shape[1]
    new_keys = fresh_all[:, :, :key_width].reshape(owned, count, KVH, HD)
    new_values = fresh_all[:, :, key_width:].reshape(owned, count, KVH, HD)
    cached = jnp.einsum("rkgd,rlkd->rkgl", query, keys, preferred_element_type=jnp.float32) * scale
    cached = jnp.where(valid, cached, -1e30)
    fresh = (
        jnp.einsum("rkgd,rjkd->rkgj", query, new_keys, preferred_element_type=jnp.float32) * scale
    )
    top = jnp.maximum(jnp.max(cached, axis=-1), jnp.max(fresh, axis=-1))
    cached_w = jnp.where(valid, jnp.exp(cached - top[..., None]), 0.0)
    fresh_w = jnp.exp(fresh - top[..., None])
    total = jnp.sum(cached_w, axis=-1) + jnp.sum(fresh_w, axis=-1)
    summed = jnp.einsum(
        "rkgl,rlkd->rkgd", cached_w.astype(jnp.bfloat16), values, preferred_element_type=jnp.float32
    )
    summed = summed + jnp.einsum(
        "rkgj,rjkd->rkgd",
        fresh_w.astype(jnp.bfloat16),
        new_values,
        preferred_element_type=jnp.float32,
    )
    attended = (summed / total[..., None]).reshape(owned, query_width).astype(jnp.bfloat16)
    delta = contract_rows(lax.all_gather(attended, ("role", "grp"), axis=0, tiled=True), w_out)
    state = state + delta[inverse]
    normed_f = full_normed(state, gain_ffn)
    gate = contract_rows(normed_f, w_gate)
    upper = contract_rows(normed_f, w_up)
    hidden = (jax.nn.silu(gate) * upper).astype(jnp.bfloat16)
    term = jnp.dot(hidden, w_down, preferred_element_type=jnp.float32)
    summed = lax.psum_scatter(term, ("role", "grp"), scatter_dimension=1, tiled=True)
    state = state + summed
    return state


def solution(mesh):
    in_specs = (
        P(None, ("role", "grp")),
        P(("role", "grp")),
        P(("role", "grp")),
        P(("role", "grp"), None),
        P(("role", "grp"), None),
        P(("role", "grp"), None),
        P(("role", "grp"), None),
        P(("role", "grp"), None),
        P(("role", "grp"), None, None),
        P(),
        P(),
    )
    out_specs = P(None, ("role", "grp"))
    return jax.shard_map(
        per_device, mesh=mesh, in_specs=in_specs, out_specs=out_specs, check_vma=False
    )
```

profile of v0, /device:TPU:24, one launch (start us, length us, event | category | flops | bytes accessed | tf_op | source)
XLA Modules:
  0.0 1463.9 jit_solution(14356021649416771107)
XLA Ops:
  6.5 0.0 copy-start
  6.5 0.0 copy-start.1
  6.5 0.0 all-gather.5.cloned.1.call-start
  6.5 0.7 all-gather.5.cloned.1.call-update
  7.3 0.0 all-reduce.5.cloned.1.call-start
  7.3 0.9 dynamic-update-slice
  8.2 0.0 copy-start.8
  8.2 0.9 dynamic-update-slice.1
  9.1 0.0 copy-start.7
  9.1 0.0 copy-done.8
  9.1 0.6 copy-done.7
  9.7 0.0 all-reduce.5.cloned.1.call-update
  9.7 0.7 compare_select_fusion.1
  10.4 3.0 fusion.31
  13.4 0.0 copy-done.1
  13.4 1.2 gather_fusion
  14.6 0.7 dynamic_slice.3
  15.3 0.0 copy-start.3
  15.3 192.8 %all-gather.5.cloned.1.call-done = f32[128,8192]{0,1:T(8,128)} async-done(((f32[128,64]{0,1:T(8,128)}), f32[128,8192]{0,1:T(8,128)}) %all-gather.5.cloned.1.call-update) | async-done | bytes 4194320 | tf_op jit(solution)/shard_map/all_gather | solution.py:50
  208.1 3.3 multiply_reduce_fusion.1
  211.4 136.7 %all-reduce.5.cloned.1.call-done = (f32[8192]{0:T(1024)}, f32[8192]{0:T(1024)}) async-done(((f32[8192]{0:T(1024)}, f32[8192]{0:T(1024)}), (f32[8192]{0:T(1024)}, f32[8192]{0:T(1024)})) %all-reduce.5.cloned.1.call-update) | async-done | bytes 65552
  348.0 0.0 copy-done
  348.0 5.0 fusion.9
  353.0 0.1 copy.23
  353.1 0.7 gather_fusion.1
  353.8 0.7 copy.24
  354.5 8.2 all-to-all-start
  362.7 0.0 all-gather.9.cloned.1.call-start
  362.7 0.6 iota_compare_fusion
  363.4 0.0 copy-done.3
  363.4 0.5 copy.37
  363.9 1.5 copy.38
  365.4 0.0 copy-start.6
  365.4 5.6 all-to-all-done
  371.1 0.2 reduce.4
  371.3 0.1 all_to_all.14
  371.4 0.1 slice_reduce_fusion
  371.5 0.1 fusion.24
  371.6 0.3 fusion.32
  372.0 0.2 fusion.12
  372.2 0.4 fusion.10
  372.6 0.6 reshape.174
  373.3 0.0 all-gather.9.cloned.1.call-update
  373.3 0.0 all-gather.7.cloned.1.call-start
  373.3 1.0 scatter_custom_fusion
  374.4 0.0 copy-start.5
  374.4 193.5 %all-gather.9.cloned.1.call-done = bf16[128,1,8192]{2,1,0:T(2,128)(2,1)} async-done(((bf16[1,1,8192]{2,1,0:T(2,128)(2,1)}), bf16[128,1,8192]{2,1,0:T(2,128)(2,1)}) %all-gather.9.cloned.1.call-update) | async-done | bytes 2097168 | tf_op jit(solution)/shard_map/all_gather | solution.py:88
  567.9 4.9 fusion.1
  572.8 0.7 gather_fusion.2
  573.4 0.1 copy.30
  573.5 0.0 copy-done.6
  573.5 0.6 add.60
  574.1 0.0 all-gather.7.cloned.1.call-update
  574.2 0.2 reduce-scatter.2.cloned.1.call-start
  574.4 196.4 %all-gather.7.cloned.1.call-done = f32[128,8192]{0,1:T(8,128)} async-done(((f32[128,64]{0,1:T(8,128)}), f32[128,8192]{0,1:T(8,128)}) %all-gather.7.cloned.1.call-update) | async-done | bytes 4194320 | tf_op jit(solution)/shard_map/all_gather | solution.py:50
  770.8 3.4 multiply_reduce_fusion
  774.2 0.0 copy-done.5
  774.2 0.0 copy-done.2
  774.2 5.2 fusion.30
  779.5 15.9 %fusion.11 = f32[128,8192]{0,1:T(8,128)} fusion(bf16[416,8192]{1,0:T(8,128)(2,1)} %param.18, bf16[416,8192]{1,0:T(8,128)(2,1)} %param.17, f32[128,416]{0,1:T(8,128)S(1)} %fusion.30, f32[128,8192]{0,1:T(8,128)} %all-gather.7.cloned.1.call-done, f32[8192]{0:T(1024)S(1)} %copy-done.5, f32[128]{0:T(128)S(1)} %add_rsqrt_fusion), kind=kOutput, calls=%fused_computation.22 | convolution fusion | flops 1748295680 | bytes 22266368 | tf_op jit(solution)/shard_map/dot_general | solution.py:94
  795.4 0.0 reduce-scatter.2.cloned.1.call-update
  795.4 660.6 %reduce-scatter.2.cloned.1.call-done = f32[128,64]{0,1:T(8,128)} async-done(((f32[128,8192]{0,1:T(8,128)}), f32[128,64]{0,1:T(8,128)}) %reduce-scatter.2.cloned.1.call-update) | async-done | bytes 32784 | tf_op jit(solution)/shard_map/reduce_scatter | solution.py:95
  1456.0 0.0 copy-done.4
  1456.0 1.4 add.63
  (14 shorter events, 0.1 us)
Async XLA Ops:
  6.5 341.5 %copy-start = (bf16[72,8192]{1,0:T(8,128)(2,1)S(1)}, bf16[72,8192]{1,0:T(8,128)(2,1)}, u32[]{:S(2)}) copy-start(bf16[72,8192]{1,0:T(8,128)(2,1)} %param.14) | copy-start | bytes 3538948
  6.5 6.8 copy-start.1
  6.5 201.5 %all-gather.5.cloned.1.call-start = ((), (), s32[]{:S(2)}) async-start(), calls=%async_computation.2 | async-start | bytes 4227072 | tf_op jit(solution)/shard_map/all_gather | solution.py:50
  7.3 340.8 %all-reduce.5.cloned.1.call-start = ((), (), s32[]{:S(2)}) async-start(), calls=%async_computation.6 | async-start | bytes 131072
  8.2 0.9 copy-start.8
  9.1 0.6 copy-start.7
  15.3 348.1 %copy-start.3 = (bf16[1,1024,512]{2,1,0:T(8,128)(2,1)S(1)}, bf16[1,1024,512]{2,1,0:T(8,128)(2,1)}, u32[]{:S(2)}) copy-start(bf16[1,1024,512]{2,1,0:T(8,128)(2,1)} %get-tuple-element.7) | copy-start | bytes 3145732
  354.5 16.6 %all-to-all-start = ((bf16[128,1,72]{2,1,0:T(2,128)(2,1)}), bf16[128,1,72]{2,1,0:T(2,128)(2,1)S(1)}, u32[]{:S(2)}, u32[]{:S(2)}) async-start(bf16[128,1,72]{2,1,0:T(2,128)(2,1)} %copy.24), calls=%async_computation | async-start | bytes 131072 | tf_op jit(solution)/shard_map/all_to_all | solution.py:59
  362.7 205.2 %all-gather.9.cloned.1.call-start = ((), (), s32[]{:S(2)}) async-start(), calls=%async_computation.5 | async-start | bytes 4227072 | tf_op jit(solution)/shard_map/all_gather | solution.py:88
  365.4 208.1 %copy-start.6 = (f32[128,64]{0,1:T(8,128)S(1)}, f32[128,64]{0,1:T(8,128)}, u32[]{:S(2)}) copy-start(f32[128,64]{0,1:T(8,128)} %param.11) | copy-start | bytes 98308
  373.3 397.5 %all-gather.7.cloned.1.call-start = ((), (), s32[]{:S(2)}) async-start(), calls=%async_computation.3 | async-start | bytes 4227072 | tf_op jit(solution)/shard_map/all_gather | solution.py:50
  374.4 399.8 %copy-start.5 = (f32[8192]{0:T(1024)S(1)}, f32[8192]{0:T(1024)}, u32[]{:S(2)}) copy-start(f32[8192]{0:T(1024)} %get-tuple-element.6) | copy-start | bytes 98308
  574.2 881.9 %reduce-scatter.2.cloned.1.call-start = ((), (), s32[]{:S(2)}) async-start(), calls=%async_computation.4 | async-start | bytes 4227072 | tf_op jit(solution)/shard_map/reduce_scatter | solution.py:95
  770.8 3.4 copy-start.2
  795.4 660.7 %copy-start.4 = (f32[128,64]{0,1:T(8,128)S(1)}, f32[128,64]{0,1:T(8,128)}, u32[]{:S(2)}) copy-start(f32[128,64]{0,1:T(8,128)} %add.60) | copy-start | bytes 98308
Sparse Core Ops, SparseCore 0:
  9.1 198.9 all-gather.4
  213.1 134.9 all-reduce.4
  373.4 194.4 all-gather.8
  574.3 196.4 all-gather.6
  795.5 660.4 reduce-scatter.1
where the time goes:
time: 1460 us
  waiting for transfers between devices  1390 us (95%)
  matrix products  31.9 us (2%)
    reduce_scatter x1, waiting for transfers between devices, per_device(): lax.psum_scatter(term, ('role', 'grp'), scatter_dimension=1, tiled=True)  661 us
    all_gather x2, waiting for transfers between devices, full_normed(): lax.all_gather(state, ('role', 'grp'), axis=1, tiled=True)  389 us
    all_gather x1, waiting for transfers between devices, per_device(): lax.all_gather(attended, ('role', 'grp'), axis=0, tiled=True)  194 us
    unnamed x6, waiting for transfers between devices  137 us
  transfers between devices with their start and end apart: 6, of which 6 were waited for; matrix products, arithmetic and copies ran while one was open for 1% of the time, Pallas kernels for 0%

commit v1 on v0

--- a/solution.py
+++ b/solution.py
@@ -47,7 +47,12 @@
 
     def full_normed(state, gain):
         whole, whole_gain = (
-            lax.all_gather(state, ("role", "grp"), axis=1, tiled=True),
+            jnp.concatenate(
+                lax.all_to_all(
+                    jnp.stack([state] * lax.axis_size(("role", "grp"))), ("role", "grp"), 0, 0
+                ),
+                axis=1,
+            ),
             lax.all_gather(gain, ("role", "grp"), axis=0, tiled=True),
         )
         mean = jnp.mean(whole * whole, axis=1, keepdims=True)

time: 1460 us -> 1170 us (0.80)
  waiting for transfers between devices: 1390 us -> 1020 us
  blocking collectives: 0 us -> 59.6 us
    all_gather x2 -> x0, waiting for transfers between devices: 389 us -> none  [full_normed(): lax.all_gather(state, ('role', 'grp'), axis=1, tiled=True)]
    all_to_all x0 -> x1, blocking collectives: none -> 59.6 us  [full_normed(): lax.all_to_all(jnp.stack([state] * lax.axis_size(('role', 'grp'))), ('rol...]
    all_to_all x0 -> x1, waiting for transfers between devices: none -> 45.9 us  [full_normed(): lax.all_to_all(jnp.stack([state] * lax.axis_size(('role', 'grp'))), ('rol...]
    unnamed x6 -> x4, waiting for transfers between devices: 137 us -> 115 us
  transfers between devices with their start and end apart: 6 -> 5, of which waited for: 6 -> 5; matrix products, arithmetic and copies ran while one was open for 1% -> 1% of each run, Pallas kernels for 0% -> 0%
where the time goes in v1:
time: 1170 us
  waiting for transfers between devices  1020 us (87%)
  blocking collectives  59.6 us (5%)
  matrix products  22.7 us (2%)
  starting transfers between devices  19 us (2%)
  local copies, waits for them, and re-layouts  15.8 us (1%)
  between operations  13.4 us (1%)
  other arithmetic  13.3 us (1%)
    reduce_scatter x1, waiting for transfers between devices, per_device(): lax.psum_scatter(term, ('role', 'grp'), scatter_dimension=1, tiled=True)  661 us
    all_gather x1, waiting for transfers between devices, per_device(): lax.all_gather(attended, ('role', 'grp'), axis=0, tiled=True)  194 us
    unnamed x4, waiting for transfers between devices  115 us
    all_to_all x1, blocking collectives, full_normed(): lax.all_to_all(jnp.stack([state] * lax.axis_size(('role', 'grp'))), ('rol...  59.6 us
    all_to_all x1, waiting for transfers between devices, full_normed(): lax.all_to_all(jnp.stack([state] * lax.axis_size(('role', 'grp'))), ('rol...  45.9 us
  transfers between devices with their start and end apart: 5, of which 5 were waited for; matrix products, arithmetic and copies ran while one was open for 1% of the time, Pallas kernels for 0%

profile of v1, /device:TPU:24, one launch (start us, length us, event | category | flops | bytes accessed | tf_op | source)
XLA Modules:
  0.0 1165.4 jit_solution(2149223802316327265)
XLA Ops:
  6.5 0.0 copy-start
  6.5 3.4 stack.6
  9.9 0.0 copy-start.6
  9.9 0.0 copy-start.7
  9.9 0.0 copy-start.8
  9.9 10.7 all-to-all-start
  20.6 0.0 all-reduce.5.cloned.1.call-start
  20.7 0.0 copy-done.6
  20.7 0.3 dynamic-update-slice
  21.0 0.0 copy-done.7
  21.0 0.3 dynamic-update-slice.1
  21.3 0.3 copy-done.4
  21.6 0.3 copy-done.3
  21.9 0.0 all-reduce.5.cloned.1.call-update
  21.9 0.0 copy-done.8
  22.0 0.0 copy-done.1
  22.0 1.2 gather_fusion
  23.2 0.7 dynamic_slice.3
  23.9 2.7 fusion.32
  26.6 45.9 %all-to-all-done = f32[128,128,64]{1,2,0:T(8,128)} async-done(((f32[128,128,64]{1,2,0:T(8,128)}), f32[128,128,64]{1,2,0:T(8,128)}, u32[]{:S(2)}, u32[]{:S(2)}) %all-to-all-start) | async-done | bytes 4194336 | tf_op jit(solution)/shard_map/all_to_all | solution.py:51
  72.4 3.3 fusion.5
  75.7 115.1 %all-reduce.5.cloned.1.call-done = (f32[8192]{0:T(1024)}, f32[8192]{0:T(1024)}) async-done(((f32[8192]{0:T(1024)}, f32[8192]{0:T(1024)}), (f32[8192]{0:T(1024)}, f32[8192]{0:T(1024)})) %all-reduce.5.cloned.1.call-update) | async-done | bytes 65552
  190.8 2.9 fusion.3
  193.7 0.0 copy-done
  193.7 0.5 convolution_convert_fusion
  194.2 0.1 copy.25
  194.3 0.7 gather_fusion.1
  195.1 0.7 copy.26
  195.7 8.2 all-to-all-start.1
  203.9 0.0 all-gather.3.cloned.1.call-start
  204.0 0.7 iota_compare_fusion
  204.7 0.5 copy.39
  205.2 1.5 copy.40
  206.7 0.0 copy-start.2
  206.7 5.6 all-to-all-done.1
  212.3 0.2 reduce.6
  212.5 0.1 all_to_all.21
  212.6 0.1 slice_reduce_fusion
  212.7 0.1 fusion.26
  212.9 0.3 fusion.33
  213.2 0.2 fusion.14
  213.4 0.4 fusion.12
  213.8 0.6 reshape.194
  214.5 0.0 all-gather.3.cloned.1.call-update
  214.5 0.0 reduce-scatter.2.cloned.1.call-start
  214.6 1.0 scatter_custom_fusion
  215.6 193.5 %all-gather.3.cloned.1.call-done = bf16[128,1,8192]{2,1,0:T(2,128)(2,1)} async-done(((bf16[1,1,8192]{2,1,0:T(2,128)(2,1)}), bf16[128,1,8192]{2,1,0:T(2,128)(2,1)}) %all-gather.3.cloned.1.call-update) | async-done | bytes 2097168 | tf_op jit(solution)/shard_map/all_gather | solution.py:93
  409.1 4.9 fusion.6
  414.0 0.7 gather_fusion.2
  414.7 0.1 copy.32
  414.7 0.0 copy-done.2
  414.8 0.5 stack.8
  415.3 0.0 slice-start
  415.3 59.6 %all_to_all.26 = f32[128,128,64]{1,2,0:T(8,128)S(1)} all-to-all(f32[128,128,64]{1,2,0:T(8,128)S(1)} %stack.8), channel_id=1, replica_groups=mesh['role'=2,'grp'=64] {'role','grp'}, dimensions={0} | all-to-all | bytes 8388608 | tf_op jit(solution)/shard_map/all_to_all | solution.py:51
  474.9 1.1 fusion.4
  476.0 0.0 copy-done.5
  476.0 3.5 fusion.1
  479.5 0.0 slice-done
  479.5 0.0 slice-done.1
  479.6 1.9 fusion.34
  481.5 14.5 %fusion.13 = f32[128,8192]{0,1:T(8,128)} fusion(bf16[416,8192]{1,0:T(8,128)(2,1)} %param.18, bf16[416,8192]{1,0:T(8,128)(2,1)} %param.17, bf16[128,8192]{0,1:T(8,128)(2,1)S(1)} %fusion.1, f32[128,416]{0,1:T(8,128)S(1)} %fusion.34), kind=kOutput, calls=%fused_computation.25 | convolution fusion | flops 1745149952 | bytes 20135936 | tf_op jit(solution)/shard_map/dot_general | solution.py:99
  496.0 0.0 reduce-scatter.2.cloned.1.call-update
  496.0 661.4 %reduce-scatter.2.cloned.1.call-done = f32[128,64]{0,1:T(8,128)} async-done(((f32[128,8192]{0,1:T(8,128)}), f32[128,64]{0,1:T(8,128)}) %reduce-scatter.2.cloned.1.call-update) | async-done | bytes 32784 | tf_op jit(solution)/shard_map/reduce_scatter | solution.py:100
  1157.5 1.4 add.63
  (20 shorter events, 0.1 us)
Async XLA Ops:
  6.5 187.2 %copy-start = (bf16[72,8192]{1,0:T(8,128)(2,1)S(1)}, bf16[72,8192]{1,0:T(8,128)(2,1)}, u32[]{:S(2)}) copy-start(bf16[72,8192]{1,0:T(8,128)(2,1)} %param.14) | copy-start | bytes 3538948
  9.9 10.8 copy-start.6
  9.9 11.1 copy-start.7
  9.9 12.0 %copy-start.8 = (s32[128]{0:T(128)S(1)}, s32[128]{0:T(128)}, u32[]{:S(2)}) copy-start(s32[128]{0:T(128)} %param.21) | copy-start | bytes 1540
  9.9 12.1 %copy-start.1 = (s32[128]{0:T(128)S(1)}, s32[128]{0:T(128)}, u32[]{:S(2)}) copy-start(s32[128]{0:T(128)} %param.20) | copy-start | bytes 1540
  9.9 62.5 %all-to-all-start = ((f32[128,128,64]{1,2,0:T(8,128)}), f32[128,128,64]{1,2,0:T(8,128)}, u32[]{:S(2)}, u32[]{:S(2)}) async-start(f32[128,128,64]{1,2,0:T(8,128)} %stack.6), calls=%async_computation | async-start | bytes 8388608 | tf_op jit(solution)/shard_map/all_to_all | solution.py:51
  20.6 170.2 %all-reduce.5.cloned.1.call-start = ((), (), s32[]{:S(2)}) async-start(), calls=%async_computation.6 | async-start | bytes 131072
  21.0 0.6 copy-start.4
  21.3 0.6 copy-start.3
  195.7 16.6 %all-to-all-start.1 = ((bf16[128,1,72]{2,1,0:T(2,128)(2,1)}), bf16[128,1,72]{2,1,0:T(2,128)(2,1)S(1)}, u32[]{:S(2)}, u32[]{:S(2)}) async-start(bf16[128,1,72]{2,1,0:T(2,128)(2,1)} %copy.26), calls=%async_computation.1 | async-start | bytes 131072 | tf_op jit(solution)/shard_map/all_to_all | solution.py:64
  203.9 205.2 %all-gather.3.cloned.1.call-start = ((), (), s32[]{:S(2)}) async-start(), calls=%async_computation.5 | async-start | bytes 4227072 | tf_op jit(solution)/shard_map/all_gather | solution.py:93
  206.7 208.0 %copy-start.2 = (f32[128,64]{0,1:T(8,128)S(1)}, f32[128,64]{0,1:T(8,128)}, u32[]{:S(2)}) copy-start(f32[128,64]{0,1:T(8,128)} %param.11) | copy-start | bytes 98308
  214.5 942.9 %reduce-scatter.2.cloned.1.call-start = ((), (), s32[]{:S(2)}) async-start(), calls=%async_computation.4 | async-start | bytes 4227072 | tf_op jit(solution)/shard_map/reduce_scatter | solution.py:100
  415.3 64.3 %slice-start = ((s8[6815744]{0:T(1024)(128)(4,1)}), s8[2621440]{0:T(1024)(128)(4,1)S(1)}, s32[]{:S(2)}) async-start(s8[6815744]{0:T(1024)(128)(4,1)} %bitcast.58), calls=%async_computation.7 | async-start | bytes 5242880
  474.9 1.1 copy-start.5
  474.9 4.6 slice-start.1
Sparse Core Ops, SparseCore 0:
  26.5 164.2 all-reduce.4
  214.6 194.4 all-gather.2
  496.1 661.2 reduce-scatter.1
